TPU v7x, 128 devices: a whole 4x4x4 slice. The times are simulated.
128 devices in a mesh: blk: 16 (over y, x_hi, core), head: 8 (over x_lo, z).
Axes of the slice: x: 4 (x_hi: 2, x_lo: 2; x = x_hi * 2 + x_lo), y: 4, z: 4, core: 2. Of those that a mesh axis runs over, the one named last changes fastest.
Arguments:
- query: bfloat16 [16384, 4096], P(('blk', 'head')), may hold values from -10 to 10
- keys: bfloat16 [16384, 1024], P(('blk', 'head')), may hold values from -10 to 10
- values: bfloat16 [16384, 1024], P(('blk', 'head')), may hold values from -6 to 6
- positions: int32 [16384], P('blk'), may hold values from 0 to 16383, as said below
Outputs:
- attended: bfloat16 [16384, 4096], P(('blk', 'head'))
Inputs may be any that keep to these rules, and one draw needn't show every extreme that they name: positions is a permutation of 0 .. 16383 made of aligned segments of 512 stored rows, each holding 512 consecutive positions in increasing order.
All inputs are finite; a program needn't handle non-finite values.
Results may differ from a plain program's by a relative error of at most 0.0065.
Values may be sent and summed in bfloat16 or wider, within the bound.
No kernel may reach another device: no remote copies, remote signals or barrier semaphores. Data moves between devices by JAX's collectives and lax.ppermute only.
A program may use at most 128 MiB of HBM per device.

v0:
```python
import math

import jax
import jax.numpy as jnp
from jax import lax
from jax.sharding import PartitionSpec as P

HEADS = 32
KV_HEADS = 8
HEAD_DIM = 128


def update(state, q_tile, q_pos, k_tile, v_tile, k_pos):
    top, total, summed = state
    scores = jnp.einsum(
        "rkgd,skd->kgrs", q_tile, k_tile, preferred_element_type=jnp.float32
    ) * HEAD_DIM ** (-0.5)
    visible = k_pos[None, :] <= q_pos[:, None]
    scores = jnp.where(visible[None, None], scores, -jnp.inf)
    new_top = jnp.maximum(top, jnp.max(scores, axis=-1))
    factor = jnp.exp(top - new_top)
    weights = jnp.exp(scores - new_top[..., None])
    new_total = total * factor + jnp.sum(weights, axis=-1)
    carried = jnp.transpose(factor, (2, 0, 1))[..., None]
    added = jnp.einsum(
        "kgrs,skd->rkgd", weights.astype(jnp.bfloat16), v_tile, preferred_element_type=jnp.float32
    )
    return (new_top, new_total, summed * carried + added)


def per_device(query, keys, values, positions):
    q_here, k_here, v_here = (
        lax.all_to_all(query, "head", split_axis=1, concat_axis=0, tiled=True),
        lax.all_to_all(keys, "head", split_axis=1, concat_axis=0, tiled=True),
        lax.all_to_all(values, "head", split_axis=1, concat_axis=0, tiled=True),
    )
    rows = q_here.shape[0]
    kv_local = k_here.shape[1] // HEAD_DIM
    group = HEADS // KV_HEADS
    q_here = q_here.reshape(rows, kv_local, group, HEAD_DIM)
    start_state = (
        jnp.full((kv_local, group, rows), -1e30, jnp.float32),
        jnp.zeros((kv_local, group, rows), jnp.float32),
        jnp.zeros((rows, kv_local, group, HEAD_DIM), jnp.float32),
    )
    k_all, v_all, p_all = (
        lax.all_gather(k_here, "blk", axis=0, tiled=True),
        lax.all_gather(v_here, "blk", axis=0, tiled=True),
        lax.all_gather(positions, "blk", axis=0, tiled=True),
    )
    k_block = k_all
    v_block = v_all
    k_poses = p_all
    count = k_block.shape[0]
    k_size = math.gcd(count, 1024)
    k_count = count // k_size
    k_block = k_block.reshape(k_count, k_size, kv_local, HEAD_DIM)
    v_block = v_block.reshape(k_count, k_size, kv_local, HEAD_DIM)
    k_poses = k_poses.reshape(k_count, k_size)

    def step(current, tiles):
        k_tile, v_tile, k_pos = tiles
        return (update(current, q_here, positions, k_tile, v_tile, k_pos), None)

    final, unused = lax.scan(step, start_state, (k_block, v_block, k_poses))
    top, total, summed = final
    scaled = summed / jnp.transpose(total, (2, 0, 1))[..., None]
    local_out = scaled.reshape(rows, kv_local * group * HEAD_DIM).astype(jnp.bfloat16)
    return lax.all_to_all(local_out, "head", split_axis=0, concat_axis=1, tiled=True)


def solution(mesh):
    placed = (
        P(("blk", "head"), None),
        P(("blk", "head"), None),
        P(("blk", "head"), None),
        P("blk"),
    )
    return jax.shard_map(
        per_device, mesh=mesh, in_specs=placed, out_specs=P(("blk", "head"), None), check_vma=False
    )
```

profile of v0, /device:TPU:1, one launch (start us, length us, event | category | flops | bytes accessed | tf_op | source)
XLA Modules:
  0.0 568.6 jit_solution(7052902479980749991)
XLA Ops:
  7.9 12.8 %all_to_all.70 = bf16[128,8,128]{2,0,1:T(8,128)(2,1)} all-to-all(bf16[128,8,128]{2,0,1:T(8,128)(2,1)S(1)} %copy.32), channel_id=1, replica_groups=mesh['blk'=16,'head'=8] {'head'}, dimensions={1} | all-to-all | bytes 524288 | tf_op jit(solution)/shard_map/all_to_all | solution.py:34
  21.9 8.5 %all_to_all.71 = bf16[128,8,128]{0,2,1:T(8,128)(2,1)S(1)} all-to-all(bf16[128,8,128]{0,2,1:T(8,128)(2,1)S(1)} %bitcast.112), channel_id=1, replica_groups=mesh['blk'=16,'head'=8] {'head'}, dimensions={1} | all-to-all | bytes 524288 | tf_op jit(solution)/shard_map/all_to_all | solution.py:35
  36.2 30.2 %all_gather.9 = s32[16384]{0:T(1024)S(1)} all-gather(s32[1024]{0:T(1024)S(1)} %copy-done.2), channel_id=1, replica_groups=mesh['blk'=16,'head'=8] {'blk'}, dimensions={0}, use_global_device_ids=true | all-gather | bytes 69632 | tf_op jit(solution)/shard_map/all_gather | solution.py:49
  68.4 8.7 %all-gather.3.cloned.1.call-done = bf16[16384,128]{1,0:T(8,128)(2,1)} async-done(((bf16[1024,128]{1,0:T(8,128)(2,1)}), bf16[16384,128]{1,0:T(8,128)(2,1)}) %all-gather.3.cloned.1.call-update) | async-done | bytes 4194320 | tf_op jit(solution)/shard_map/all_gather | solution.py:47
  77.1 55.6 %all-gather.5.cloned.1.call-done = bf16[16384,128]{1,0:T(8,128)(2,1)} async-done(((bf16[1024,128]{1,0:T(8,128)(2,1)}), bf16[16384,128]{1,0:T(8,128)(2,1)}) %all-gather.5.cloned.1.call-update) | async-done | bytes 4194320 | tf_op jit(solution)/shard_map/all_gather | solution.py:48
  132.6 406.1 %while.15 = (s32[]{:T(128)}, f32[1,4,1024]{2,1,0:T(4,128)S(1)}, f32[1,4,1024]{2,1,0:T(4,128)S(1)}, f32[1024,1,4,128]{0,3,2,1:T(8,128)}, s32[16,1024]{1,0:T(8,128...) while((s32[]{:T(128)}, f32[1,4,1024]{2,1,0:T(4,128)S(1)}, ...), condition=%wide.region_3.4_spmd.clone, body=%wide.region_0.3_spmd.clone.sunk | while | flops 2196267008 | bytes 127681688 | solution.py:65
  141.6 12.2 %bitcast_add_fusion.5 = f32[1024,1,4,128]{0,3,2,1:T(8,128)} fusion(f32[1024,1,4,128]{0,3,2,1:T(8,128)} %get-tuple-element.220, f32[1024,1024,4]{1,0,2:T(8,128)} %get-tuple-element.204, f32[4,1024]{1,0:T(4,128)S(1)} %bitcast.102, pred[1024,1024]{0,1:T(8,128)(4,1)S(1)} %broadcast_compare_fusion.2, f32[1024,4]{0,1:T(4,128)S(1)} %get-tuple-element.205, ...), kind=kOutput, calls=%fused_computation.8.clone.1 | convolution fusion | flops 1092091904 | bytes 22315520 | tf_op jit(solution)/shard_map/while/body/eval_jaxpr/kgrs,skd->rkgd/dot_general | solution.py:25
  158.1 8.3 %fusion.27 = (f32[4,1024]{1,0:T(4,128)S(1)}, f32[1024,1024,4]{1,0,2:T(8,128)}) fusion(pred[1024,1024]{0,1:T(8,128)(4,1)S(1)} %broadcast_compare_fusion.2, bf16[1024,1,4,128]{3,0,2,1:T(8,128)(2,1)S(1)} %get-tuple-element.235, bf16[16,1024,1,128]{3,1,2,0:T(8,128)(2,1)} %get-tuple-element.234, s32[]{:T(128)} %get-tuple-element.217), kind=kOutput, calls=%fused_computation.4.clone.1 | convolution fusion | flops 1086320640 | bytes 19153408 | tf_op jit(solution)/shard_map/while/body/eval_jaxpr/rkgd,skd->kgrs/dot_general | solution.py:15
  166.4 12.8 %bitcast_add_fusion.5 = f32[1024,1,4,128]{0,3,2,1:T(8,128)} fusion(f32[1024,1,4,128]{0,3,2,1:T(8,128)} %get-tuple-element.220, f32[1024,1024,4]{1,0,2:T(8,128)} %get-tuple-element.204, f32[4,1024]{1,0:T(4,128)S(1)} %bitcast.102, pred[1024,1024]{0,1:T(8,128)(4,1)S(1)} %broadcast_compare_fusion.2, f32[1024,4]{0,1:T(4,128)S(1)} %get-tuple-element.205, ...), kind=kOutput, calls=%fused_computation.8.clone.1 | convolution fusion | flops 1092091904 | bytes 22315520 | tf_op jit(solution)/shard_map/while/body/eval_jaxpr/kgrs,skd->rkgd/dot_general | solution.py:25
  191.8 12.7 %bitcast_add_fusion.5 = f32[1024,1,4,128]{0,3,2,1:T(8,128)} fusion(f32[1024,1,4,128]{0,3,2,1:T(8,128)} %get-tuple-element.220, f32[1024,1024,4]{1,0,2:T(8,128)} %get-tuple-element.204, f32[4,1024]{1,0:T(4,128)S(1)} %bitcast.102, pred[1024,1024]{0,1:T(8,128)(4,1)S(1)} %broadcast_compare_fusion.2, f32[1024,4]{0,1:T(4,128)S(1)} %get-tuple-element.205, ...), kind=kOutput, calls=%fused_computation.8.clone.1 | convolution fusion | flops 1092091904 | bytes 22315520 | tf_op jit(solution)/shard_map/while/body/eval_jaxpr/kgrs,skd->rkgd/dot_general | solution.py:25
  217.3 12.8 %bitcast_add_fusion.5 = f32[1024,1,4,128]{0,3,2,1:T(8,128)} fusion(f32[1024,1,4,128]{0,3,2,1:T(8,128)} %get-tuple-element.220, f32[1024,1024,4]{1,0,2:T(8,128)} %get-tuple-element.204, f32[4,1024]{1,0:T(4,128)S(1)} %bitcast.102, pred[1024,1024]{0,1:T(8,128)(4,1)S(1)} %broadcast_compare_fusion.2, f32[1024,4]{0,1:T(4,128)S(1)} %get-tuple-element.205, ...), kind=kOutput, calls=%fused_computation.8.clone.1 | convolution fusion | flops 1092091904 | bytes 22315520 | tf_op jit(solution)/shard_map/while/body/eval_jaxpr/kgrs,skd->rkgd/dot_general | solution.py:25
  242.7 12.7 %bitcast_add_fusion.5 = f32[1024,1,4,128]{0,3,2,1:T(8,128)} fusion(f32[1024,1,4,128]{0,3,2,1:T(8,128)} %get-tuple-element.220, f32[1024,1024,4]{1,0,2:T(8,128)} %get-tuple-element.204, f32[4,1024]{1,0:T(4,128)S(1)} %bitcast.102, pred[1024,1024]{0,1:T(8,128)(4,1)S(1)} %broadcast_compare_fusion.2, f32[1024,4]{0,1:T(4,128)S(1)} %get-tuple-element.205, ...), kind=kOutput, calls=%fused_computation.8.clone.1 | convolution fusion | flops 1092091904 | bytes 22315520 | tf_op jit(solution)/shard_map/while/body/eval_jaxpr/kgrs,skd->rkgd/dot_general | solution.py:25
  268.1 12.8 %bitcast_add_fusion.5 = f32[1024,1,4,128]{0,3,2,1:T(8,128)} fusion(f32[1024,1,4,128]{0,3,2,1:T(8,128)} %get-tuple-element.220, f32[1024,1024,4]{1,0,2:T(8,128)} %get-tuple-element.204, f32[4,1024]{1,0:T(4,128)S(1)} %bitcast.102, pred[1024,1024]{0,1:T(8,128)(4,1)S(1)} %broadcast_compare_fusion.2, f32[1024,4]{0,1:T(4,128)S(1)} %get-tuple-element.205, ...), kind=kOutput, calls=%fused_computation.8.clone.1 | convolution fusion | flops 1092091904 | bytes 22315520 | tf_op jit(solution)/shard_map/while/body/eval_jaxpr/kgrs,skd->rkgd/dot_general | solution.py:25
  293.5 12.7 %bitcast_add_fusion.5 = f32[1024,1,4,128]{0,3,2,1:T(8,128)} fusion(f32[1024,1,4,128]{0,3,2,1:T(8,128)} %get-tuple-element.220, f32[1024,1024,4]{1,0,2:T(8,128)} %get-tuple-element.204, f32[4,1024]{1,0:T(4,128)S(1)} %bitcast.102, pred[1024,1024]{0,1:T(8,128)(4,1)S(1)} %broadcast_compare_fusion.2, f32[1024,4]{0,1:T(4,128)S(1)} %get-tuple-element.205, ...), kind=kOutput, calls=%fused_computation.8.clone.1 | convolution fusion | flops 1092091904 | bytes 22315520 | tf_op jit(solution)/shard_map/while/body/eval_jaxpr/kgrs,skd->rkgd/dot_general | solution.py:25
  318.9 12.8 %bitcast_add_fusion.5 = f32[1024,1,4,128]{0,3,2,1:T(8,128)} fusion(f32[1024,1,4,128]{0,3,2,1:T(8,128)} %get-tuple-element.220, f32[1024,1024,4]{1,0,2:T(8,128)} %get-tuple-element.204, f32[4,1024]{1,0:T(4,128)S(1)} %bitcast.102, pred[1024,1024]{0,1:T(8,128)(4,1)S(1)} %broadcast_compare_fusion.2, f32[1024,4]{0,1:T(4,128)S(1)} %get-tuple-element.205, ...), kind=kOutput, calls=%fused_computation.8.clone.1 | convolution fusion | flops 1092091904 | bytes 22315520 | tf_op jit(solution)/shard_map/while/body/eval_jaxpr/kgrs,skd->rkgd/dot_general | solution.py:25
  344.3 12.7 %bitcast_add_fusion.5 = f32[1024,1,4,128]{0,3,2,1:T(8,128)} fusion(f32[1024,1,4,128]{0,3,2,1:T(8,128)} %get-tuple-element.220, f32[1024,1024,4]{1,0,2:T(8,128)} %get-tuple-element.204, f32[4,1024]{1,0:T(4,128)S(1)} %bitcast.102, pred[1024,1024]{0,1:T(8,128)(4,1)S(1)} %broadcast_compare_fusion.2, f32[1024,4]{0,1:T(4,128)S(1)} %get-tuple-element.205, ...), kind=kOutput, calls=%fused_computation.8.clone.1 | convolution fusion | flops 1092091904 | bytes 22315520 | tf_op jit(solution)/shard_map/while/body/eval_jaxpr/kgrs,skd->rkgd/dot_general | solution.py:25
  369.8 12.8 %bitcast_add_fusion.5 = f32[1024,1,4,128]{0,3,2,1:T(8,128)} fusion(f32[1024,1,4,128]{0,3,2,1:T(8,128)} %get-tuple-element.220, f32[1024,1024,4]{1,0,2:T(8,128)} %get-tuple-element.204, f32[4,1024]{1,0:T(4,128)S(1)} %bitcast.102, pred[1024,1024]{0,1:T(8,128)(4,1)S(1)} %broadcast_compare_fusion.2, f32[1024,4]{0,1:T(4,128)S(1)} %get-tuple-element.205, ...), kind=kOutput, calls=%fused_computation.8.clone.1 | convolution fusion | flops 1092091904 | bytes 22315520 | tf_op jit(solution)/shard_map/while/body/eval_jaxpr/kgrs,skd->rkgd/dot_general | solution.py:25
  395.2 12.7 %bitcast_add_fusion.5 = f32[1024,1,4,128]{0,3,2,1:T(8,128)} fusion(f32[1024,1,4,128]{0,3,2,1:T(8,128)} %get-tuple-element.220, f32[1024,1024,4]{1,0,2:T(8,128)} %get-tuple-element.204, f32[4,1024]{1,0:T(4,128)S(1)} %bitcast.102, pred[1024,1024]{0,1:T(8,128)(4,1)S(1)} %broadcast_compare_fusion.2, f32[1024,4]{0,1:T(4,128)S(1)} %get-tuple-element.205, ...), kind=kOutput, calls=%fused_computation.8.clone.1 | convolution fusion | flops 1092091904 | bytes 22315520 | tf_op jit(solution)/shard_map/while/body/eval_jaxpr/kgrs,skd->rkgd/dot_general | solution.py:25
  420.6 12.8 %bitcast_add_fusion.5 = f32[1024,1,4,128]{0,3,2,1:T(8,128)} fusion(f32[1024,1,4,128]{0,3,2,1:T(8,128)} %get-tuple-element.220, f32[1024,1024,4]{1,0,2:T(8,128)} %get-tuple-element.204, f32[4,1024]{1,0:T(4,128)S(1)} %bitcast.102, pred[1024,1024]{0,1:T(8,128)(4,1)S(1)} %broadcast_compare_fusion.2, f32[1024,4]{0,1:T(4,128)S(1)} %get-tuple-element.205, ...), kind=kOutput, calls=%fused_computation.8.clone.1 | convolution fusion | flops 1092091904 | bytes 22315520 | tf_op jit(solution)/shard_map/while/body/eval_jaxpr/kgrs,skd->rkgd/dot_general | solution.py:25
  446.0 12.7 %bitcast_add_fusion.5 = f32[1024,1,4,128]{0,3,2,1:T(8,128)} fusion(f32[1024,1,4,128]{0,3,2,1:T(8,128)} %get-tuple-element.220, f32[1024,1024,4]{1,0,2:T(8,128)} %get-tuple-element.204, f32[4,1024]{1,0:T(4,128)S(1)} %bitcast.102, pred[1024,1024]{0,1:T(8,128)(4,1)S(1)} %broadcast_compare_fusion.2, f32[1024,4]{0,1:T(4,128)S(1)} %get-tuple-element.205, ...), kind=kOutput, calls=%fused_computation.8.clone.1 | convolution fusion | flops 1092091904 | bytes 22315520 | tf_op jit(solution)/shard_map/while/body/eval_jaxpr/kgrs,skd->rkgd/dot_general | solution.py:25
  471.4 12.8 %bitcast_add_fusion.5 = f32[1024,1,4,128]{0,3,2,1:T(8,128)} fusion(f32[1024,1,4,128]{0,3,2,1:T(8,128)} %get-tuple-element.220, f32[1024,1024,4]{1,0,2:T(8,128)} %get-tuple-element.204, f32[4,1024]{1,0:T(4,128)S(1)} %bitcast.102, pred[1024,1024]{0,1:T(8,128)(4,1)S(1)} %broadcast_compare_fusion.2, f32[1024,4]{0,1:T(4,128)S(1)} %get-tuple-element.205, ...), kind=kOutput, calls=%fused_computation.8.clone.1 | convolution fusion | flops 1092091904 | bytes 22315520 | tf_op jit(solution)/shard_map/while/body/eval_jaxpr/kgrs,skd->rkgd/dot_general | solution.py:25
  496.9 12.7 %bitcast_add_fusion.5 = f32[1024,1,4,128]{0,3,2,1:T(8,128)} fusion(f32[1024,1,4,128]{0,3,2,1:T(8,128)} %get-tuple-element.220, f32[1024,1024,4]{1,0,2:T(8,128)} %get-tuple-element.204, f32[4,1024]{1,0:T(4,128)S(1)} %bitcast.102, pred[1024,1024]{0,1:T(8,128)(4,1)S(1)} %broadcast_compare_fusion.2, f32[1024,4]{0,1:T(4,128)S(1)} %get-tuple-element.205, ...), kind=kOutput, calls=%fused_computation.8.clone.1 | convolution fusion | flops 1092091904 | bytes 22315520 | tf_op jit(solution)/shard_map/while/body/eval_jaxpr/kgrs,skd->rkgd/dot_general | solution.py:25
  522.3 12.8 %bitcast_add_fusion.5 = f32[1024,1,4,128]{0,3,2,1:T(8,128)} fusion(f32[1024,1,4,128]{0,3,2,1:T(8,128)} %get-tuple-element.220, f32[1024,1024,4]{1,0,2:T(8,128)} %get-tuple-element.204, f32[4,1024]{1,0:T(4,128)S(1)} %bitcast.102, pred[1024,1024]{0,1:T(8,128)(4,1)S(1)} %broadcast_compare_fusion.2, f32[1024,4]{0,1:T(4,128)S(1)} %get-tuple-element.205, ...), kind=kOutput, calls=%fused_computation.8.clone.1 | convolution fusion | flops 1092091904 | bytes 22315520 | tf_op jit(solution)/shard_map/while/body/eval_jaxpr/kgrs,skd->rkgd/dot_general | solution.py:25
  541.6 18.3 %all_to_all.72 = bf16[8,128,512]{2,1,0:T(8,128)(2,1)S(1)} all-to-all(bf16[8,128,512]{2,1,0:T(8,128)(2,1)S(1)} %copy.43), channel_id=1, replica_groups=mesh['blk'=16,'head'=8] {'head'}, dimensions={0} | all-to-all | bytes 2097152 | tf_op jit(solution)/shard_map/all_to_all | solution.py:69
  (170 shorter events, 208.5 us)
Async XLA Ops:
  6.5 24.8 %copy-start.1 = (bf16[128,4096]{1,0:T(8,128)(2,1)S(1)}, bf16[128,4096]{1,0:T(8,128)(2,1)}, u32[]{:S(2)}) copy-start(bf16[128,4096]{1,0:T(8,128)(2,1)} %param.6) | copy-start | bytes 3145732
  6.5 29.7 %copy-start.2 = (s32[1024]{0:T(1024)S(1)}, s32[1024]{0:T(1024)}, u32[]{:S(2)}) copy-start(s32[1024]{0:T(1024)} %param.9) | copy-start | bytes 12292
  6.5 70.5 %all-gather.3.cloned.1.call-start = ((), (), s32[]{:S(2)}) async-start(), calls=%async_computation.4 | async-start | bytes 4456448 | tf_op jit(solution)/shard_map/all_gather | solution.py:47
  20.8 111.8 %all-gather.5.cloned.1.call-start = ((), (), s32[]{:S(2)}) async-start(), calls=%async_computation.5 | async-start | bytes 4456448 | tf_op jit(solution)/shard_map/all_gather | solution.py:48
  32.6 33.9 %all-to-all-start.1 = ((bf16[128,8,512]{0,2,1:T(8,128)(2,1)}), bf16[128,8,512]{0,2,1:T(8,128)(2,1)S(1)}, u32[]{:S(2)}, u32[]{:S(2)}) async-start(bf16[128,8,512]{0,2,1:T(8,128)(2,1)} %bitcast.4), calls=%async_computation.1 | async-start | bytes 2097152 | tf_op jit(solution)/shard_map/all_to_all | solution.py:33
  141.6 12.2 %copy-start = (f32[1024,1024,4]{1,0,2:T(8,128)S(1)}, f32[1024,1024,4]{1,0,2:T(8,128)}, u32[]{:S(2)}) copy-start(f32[1024,1024,4]{1,0,2:T(8,128)} %get-tuple-element.204) | copy-start | bytes 50331652 | tf_op jit(solution)/shard_map/while
  166.4 12.8 %copy-start = (f32[1024,1024,4]{1,0,2:T(8,128)S(1)}, f32[1024,1024,4]{1,0,2:T(8,128)}, u32[]{:S(2)}) copy-start(f32[1024,1024,4]{1,0,2:T(8,128)} %get-tuple-element.204) | copy-start | bytes 50331652 | tf_op jit(solution)/shard_map/while
  191.8 12.8 %copy-start = (f32[1024,1024,4]{1,0,2:T(8,128)S(1)}, f32[1024,1024,4]{1,0,2:T(8,128)}, u32[]{:S(2)}) copy-start(f32[1024,1024,4]{1,0,2:T(8,128)} %get-tuple-element.204) | copy-start | bytes 50331652 | tf_op jit(solution)/shard_map/while
  217.2 12.8 %copy-start = (f32[1024,1024,4]{1,0,2:T(8,128)S(1)}, f32[1024,1024,4]{1,0,2:T(8,128)}, u32[]{:S(2)}) copy-start(f32[1024,1024,4]{1,0,2:T(8,128)} %get-tuple-element.204) | copy-start | bytes 50331652 | tf_op jit(solution)/shard_map/while
  242.7 12.8 %copy-start = (f32[1024,1024,4]{1,0,2:T(8,128)S(1)}, f32[1024,1024,4]{1,0,2:T(8,128)}, u32[]{:S(2)}) copy-start(f32[1024,1024,4]{1,0,2:T(8,128)} %get-tuple-element.204) | copy-start | bytes 50331652 | tf_op jit(solution)/shard_map/while
  268.1 12.8 %copy-start = (f32[1024,1024,4]{1,0,2:T(8,128)S(1)}, f32[1024,1024,4]{1,0,2:T(8,128)}, u32[]{:S(2)}) copy-start(f32[1024,1024,4]{1,0,2:T(8,128)} %get-tuple-element.204) | copy-start | bytes 50331652 | tf_op jit(solution)/shard_map/while
  293.5 12.8 %copy-start = (f32[1024,1024,4]{1,0,2:T(8,128)S(1)}, f32[1024,1024,4]{1,0,2:T(8,128)}, u32[]{:S(2)}) copy-start(f32[1024,1024,4]{1,0,2:T(8,128)} %get-tuple-element.204) | copy-start | bytes 50331652 | tf_op jit(solution)/shard_map/while
  318.9 12.8 %copy-start = (f32[1024,1024,4]{1,0,2:T(8,128)S(1)}, f32[1024,1024,4]{1,0,2:T(8,128)}, u32[]{:S(2)}) copy-start(f32[1024,1024,4]{1,0,2:T(8,128)} %get-tuple-element.204) | copy-start | bytes 50331652 | tf_op jit(solution)/shard_map/while
  344.3 12.8 %copy-start = (f32[1024,1024,4]{1,0,2:T(8,128)S(1)}, f32[1024,1024,4]{1,0,2:T(8,128)}, u32[]{:S(2)}) copy-start(f32[1024,1024,4]{1,0,2:T(8,128)} %get-tuple-element.204) | copy-start | bytes 50331652 | tf_op jit(solution)/shard_map/while
  369.8 12.8 %copy-start = (f32[1024,1024,4]{1,0,2:T(8,128)S(1)}, f32[1024,1024,4]{1,0,2:T(8,128)}, u32[]{:S(2)}) copy-start(f32[1024,1024,4]{1,0,2:T(8,128)} %get-tuple-element.204) | copy-start | bytes 50331652 | tf_op jit(solution)/shard_map/while
  395.2 12.8 %copy-start = (f32[1024,1024,4]{1,0,2:T(8,128)S(1)}, f32[1024,1024,4]{1,0,2:T(8,128)}, u32[]{:S(2)}) copy-start(f32[1024,1024,4]{1,0,2:T(8,128)} %get-tuple-element.204) | copy-start | bytes 50331652 | tf_op jit(solution)/shard_map/while
  420.6 12.8 %copy-start = (f32[1024,1024,4]{1,0,2:T(8,128)S(1)}, f32[1024,1024,4]{1,0,2:T(8,128)}, u32[]{:S(2)}) copy-start(f32[1024,1024,4]{1,0,2:T(8,128)} %get-tuple-element.204) | copy-start | bytes 50331652 | tf_op jit(solution)/shard_map/while
  446.0 12.8 %copy-start = (f32[1024,1024,4]{1,0,2:T(8,128)S(1)}, f32[1024,1024,4]{1,0,2:T(8,128)}, u32[]{:S(2)}) copy-start(f32[1024,1024,4]{1,0,2:T(8,128)} %get-tuple-element.204) | copy-start | bytes 50331652 | tf_op jit(solution)/shard_map/while
  471.4 12.8 %copy-start = (f32[1024,1024,4]{1,0,2:T(8,128)S(1)}, f32[1024,1024,4]{1,0,2:T(8,128)}, u32[]{:S(2)}) copy-start(f32[1024,1024,4]{1,0,2:T(8,128)} %get-tuple-element.204) | copy-start | bytes 50331652 | tf_op jit(solution)/shard_map/while
  496.8 12.8 %copy-start = (f32[1024,1024,4]{1,0,2:T(8,128)S(1)}, f32[1024,1024,4]{1,0,2:T(8,128)}, u32[]{:S(2)}) copy-start(f32[1024,1024,4]{1,0,2:T(8,128)} %get-tuple-element.204) | copy-start | bytes 50331652 | tf_op jit(solution)/shard_map/while
  522.3 12.8 %copy-start = (f32[1024,1024,4]{1,0,2:T(8,128)S(1)}, f32[1024,1024,4]{1,0,2:T(8,128)}, u32[]{:S(2)}) copy-start(f32[1024,1024,4]{1,0,2:T(8,128)} %get-tuple-element.204) | copy-start | bytes 50331652 | tf_op jit(solution)/shard_map/while
Sparse Core Ops, SparseCore 0:
  20.9 56.1 all-gather.2
  79.5 53.0 all-gather.4
where the time goes:
time: 570 us; the launch traced here: 569 us
  matrix products  336 us (59%)
  other arithmetic  71.2 us (12%)
  blocking collectives  69.8 us (12%)
  waiting for transfers between devices  64.3 us (11%)
  between operations  13.5 us (2%)
  local copies, waits for them, and re-layouts  9.74 us (2%)
    dot_general x16, matrix products, update(): jnp.einsum('kgrs,skd->rkgd', weights.astype(jnp.bfloat16), v_tile, prefer...  203 us
    dot_general x16, matrix products, update(): jnp.einsum('rkgd,skd->kgrs', q_tile, k_tile, preferred_element_type=jnp.f...  132 us
    reduce_sum x16, other arithmetic, update(): new_total = total * factor + jnp.sum(weights, axis=-1)  58.1 us
    all_gather x1, waiting for transfers between devices, per_device(): lax.all_gather(v_here, 'blk', axis=0, tiled=True)  55.6 us
    all_gather x1, blocking collectives, per_device(): lax.all_gather(positions, 'blk', axis=0, tiled=True)  30.2 us
    all_to_all x1, blocking collectives, per_device(): lax.all_to_all(local_out, 'head', split_axis=0, concat_axis=1, tiled=True)  18.3 us
    all_to_all x1, blocking collectives, per_device(): lax.all_to_all(keys, 'head', split_axis=1, concat_axis=0, tiled=True)  12.8 us
  transfers between devices with their start and end apart: 3, of which 2 were waited for; matrix products, arithmetic and copies ran while one was open for 1% of the time, Pallas kernels for 0%

commit v1 on v0

v1 whole, which is shorter than its diff:
```python
import functools

import jax
import jax.numpy as jnp
from jax import lax
from jax.experimental import pallas as pl
from jax.experimental.pallas import tpu as pltpu
from jax.sharding import PartitionSpec as P

HEADS = 32
KV_HEADS = 8
HEAD_DIM = 128
GROUP = HEADS // KV_HEADS
SEGLEN = 512
SEGS = 32
PART = SEGLEN // 16
TILE = GROUP * PART
ROWS = SEGS * TILE
QB = 512
QSEGS = QB // TILE
QBLOCKS = ROWS // QB
LOG2E = 1.4426950408889634
SCALE = HEAD_DIM**-0.5 * LOG2E
LOW = -1e30
UNROLL = 4
NT = (((1,), (1,)), ((), ()))
bf16, f32, i32 = jnp.bfloat16, jnp.float32, jnp.int32


def attend(sizes, first, last, *refs):
    n_seg = sum(sizes)
    refs = list(refs)
    meta, q_ref = refs[:2]
    refs = refs[2:]
    state_in = None if first else refs.pop(0)
    chunks, refs = refs[: len(sizes)], refs[len(sizes) :]
    if first:
        qs, state_out = refs[:2]
        refs = refs[2:]
    elif last:
        qs, out = q_ref, refs.pop(0)
    else:
        qs, state_out = q_ref, refs.pop(0)
    kv, m_ref, l_ref, acc, s_scr, p_scr, a_scr, base, st_e, st_r, st_p, sems = refs
    state = (m_ref, l_ref, acc)

    copies, start = [], 0
    for index, size in enumerate(sizes):
        copies.append(pltpu.make_async_copy(chunks[index], kv.at[pl.ds(start, size)], sems.at[index]))
        start += size
    if not first:
        for index, ref in enumerate(state):
            copies.append(
                pltpu.make_async_copy(state_in.at[index], ref.at[pl.ds(0, ROWS)], sems.at[len(sizes) + index])
            )
    for copy in copies:
        copy.start()

    def masked_step(e, _):
        p = meta[meta[SEGS + e]]
        st_e[1 + e] = e
        st_r[1 + e] = lax.div(p, QSEGS)
        st_p[1 + e] = p
        return 0

    lax.fori_loop(0, n_seg, masked_step, 0)

    def full_steps(e, count):
        def one(r, count):
            st_e[count] = e
            st_r[count] = r
            return count + 1

        return lax.fori_loop(st_r[1 + e] + 1, QBLOCKS, one, count)

    count = lax.fori_loop(0, n_seg, full_steps, 1 + n_seg)
    for index in [0] + [count + i for i in range(UNROLL + 2)]:
        st_e[index] = 0
        st_r[index] = QBLOCKS

    row = lax.broadcasted_iota(i32, (QB, 128), 0)
    lane = lax.broadcasted_iota(i32, (QB, 128), 1)
    within = lax.rem(row, TILE)
    place = lax.rem(within, PART)
    base[...] = (
        lax.div(row, TILE) * SEGLEN + lax.div(place, 8) * 128 + lax.rem(place, 8) + meta[2 * SEGS] - lane
    )

    if first:
        def stack(s, _):
            p = meta[s]
            for g in range(GROUP):
                to = pl.multiple_of(p * TILE + g * PART, PART)
                qs[pl.ds(to, PART), :] = q_ref[
                    pl.ds(pl.multiple_of(s * PART, PART), PART), g * HEAD_DIM : (g + 1) * HEAD_DIM
                ]
            return 0

        lax.fori_loop(0, SEGS, stack, 0)
        qs[pl.ds(ROWS, QB), :] = jnp.zeros((QB, HEAD_DIM), bf16)
        m_ref[...] = jnp.full_like(m_ref, LOW)
        l_ref[...] = jnp.zeros_like(l_ref)
        acc[...] = jnp.zeros_like(acc)
    p_scr[0] = jnp.zeros((QB, SEGLEN), bf16)
    a_scr[0] = jnp.zeros((QB, 128), f32)

    for copy in copies:
        copy.wait()

    def rows_of(t):
        return pl.ds(pl.multiple_of(st_r[t] * QB, QB), QB)

    def scores(t, slot):
        s_scr[slot] = lax.dot_general(
            qs[rows_of(t), :], kv[st_e[t], :, :HEAD_DIM], NT, preferred_element_type=f32
        )

    def soften(t, slot, masked):
        rows = rows_of(t)
        pieces = range(0, SEGLEN, 128)
        if masked:
            shift = (st_p[t] - st_r[t] * QSEGS) * SEGLEN
            for c in pieces:
                s_scr[slot, :, c : c + 128] = jnp.where(
                    base[...] >= shift + c, s_scr[slot, :, c : c + 128], LOW
                )
        top = s_scr[slot, :, 0:128]
        for c in pieces[1:]:
            top = jnp.maximum(top, s_scr[slot, :, c : c + 128])
        before = m_ref[rows, :]
        now = jnp.maximum(before, jnp.max(top, axis=1, keepdims=True) * SCALE)
        factor = jnp.exp2(before - now)
        m_ref[rows, :] = now
        a_scr[slot] = factor
        total = l_ref[rows, :] * factor
        for c in pieces:
            weight = jnp.exp2(s_scr[slot, :, c : c + 128] * SCALE - now)
            total = total + weight
            p_scr[slot, :, c : c + 128] = weight.astype(bf16)
        l_ref[rows, :] = total

    def gather(t, slot):
        rows = rows_of(t)
        added = jnp.dot(p_scr[slot], kv[st_e[t], :, HEAD_DIM:], preferred_element_type=f32)
        acc[rows, :] = acc[rows, :] * a_scr[slot] + added

    def steps(masked, offset):
        def body(u, _):
            for r in range(UNROLL):
                t = offset + u * UNROLL + r
                slot = (offset + r) % 2
                gather(t - 1, 1 - slot)
                soften(t, slot, masked)
                scores(t + 1, 1 - slot)
            return 0

        return body

    assert n_seg % UNROLL == 0
    scores(1, 1)
    lax.fori_loop(0, n_seg // UNROLL, steps(True, 1), 0)
    left = count - n_seg
    lax.fori_loop(0, lax.div(left + UNROLL - 1, UNROLL), steps(False, 1 + n_seg), 0)

    if last:
        def finish(s, _):
            p = meta[s]
            for g in range(GROUP):
                rows = pl.ds(pl.multiple_of(p * TILE + g * PART, PART), PART)
                total = jnp.sum(l_ref[rows, :], axis=1, keepdims=True)
                out[pl.ds(pl.multiple_of(s * PART, PART), PART), g * HEAD_DIM : (g + 1) * HEAD_DIM] = (
                    acc[rows, :] / total
                ).astype(bf16)
            return 0

        lax.fori_loop(0, SEGS, finish, 0)
    else:
        copies = [
            pltpu.make_async_copy(ref.at[pl.ds(0, ROWS)], state_out.at[index], sems.at[index])
            for index, ref in enumerate(state)
        ]
        for copy in copies:
            copy.start()
        for copy in copies:
            copy.wait()


def attention_call(order, mine, blocks, q, state, chunks, last):
    first = state is None
    chunks = [c.reshape(-1, SEGLEN, 2 * HEAD_DIM) for c in chunks]
    sizes = [c.shape[0] for c in chunks]
    n_seg = sum(sizes)
    segments = jnp.stack([jnp.stack([2 * b, 2 * b + 1]) for b in blocks]).reshape(-1)
    segments = jnp.pad(segments, (0, SEGS - n_seg))
    meta = jnp.concatenate([order, segments, jnp.full((8,), mine * 8, i32)])
    vmem, hbm = pl.BlockSpec(memory_space=pltpu.VMEM), pl.BlockSpec(memory_space=pl.ANY)
    operands = [meta, q] + ([] if first else [state]) + chunks
    in_specs = [pl.BlockSpec(memory_space=pltpu.SMEM), vmem] + [hbm] * (len(operands) - 2)
    stacked = jax.ShapeDtypeStruct((ROWS + QB, HEAD_DIM), bf16)
    saved = jax.ShapeDtypeStruct((3, ROWS, 128), f32)
    if first:
        out_shape, out_specs = (stacked, saved), (vmem, hbm)
    elif last:
        out_shape, out_specs = jax.ShapeDtypeStruct((SEGS * PART, GROUP * HEAD_DIM), bf16), vmem
    else:
        out_shape, out_specs = saved, hbm
    steps = n_seg * 9 // 2 + n_seg // 2
    return pl.pallas_call(
        functools.partial(attend, sizes, first, last),
        out_shape=out_shape,
        in_specs=in_specs,
        out_specs=out_specs,
        scratch_shapes=[
            pltpu.VMEM((n_seg, SEGLEN, 2 * HEAD_DIM), bf16),
            pltpu.VMEM((ROWS + QB, 128), f32),
            pltpu.VMEM((ROWS + QB, 128), f32),
            pltpu.VMEM((ROWS + QB, 128), f32),
            pltpu.VMEM((2, QB, SEGLEN), f32),
            pltpu.VMEM((2, QB, SEGLEN), bf16),
            pltpu.VMEM((2, QB, 128), f32),
            pltpu.VMEM((QB, 128), i32),
            pltpu.SMEM((n_seg * (QBLOCKS + 1) + 16,), i32),
            pltpu.SMEM((n_seg * (QBLOCKS + 1) + 16,), i32),
            pltpu.SMEM((n_seg * (QBLOCKS + 1) + 16,), i32),
            pltpu.SemaphoreType.DMA((len(sizes) + 3,)),
        ],
        compiler_params=pltpu.CompilerParams(vmem_limit_bytes=40 * 2**20),
        cost_estimate=pl.CostEstimate(
            flops=steps * QB * SEGLEN * 4 * HEAD_DIM,
            bytes_accessed=n_seg * SEGLEN * 512 + ROWS * 128 * 24,
            transcendentals=steps * QB * SEGLEN,
        ),
    )(*operands)


def moved(x, dy, dx, dcore):
    pairs = []
    for y in range(4):
        for x_hi in range(2):
            for core in range(2):
                to = ((y + dy) % 4) * 4 + (x_hi ^ dx) * 2 + (core ^ dcore)
                pairs.append((y * 4 + x_hi * 2 + core, to))
    return lax.ppermute(x, "blk", pairs)


def per_device(query, keys, values, positions):
    n_blk, n_head = lax.axis_size("blk"), lax.axis_size("head")
    blk, head = lax.axis_index("blk"), lax.axis_index("head")
    rows = query.shape[0]
    quarters = SEGLEN // rows

    both = jnp.concatenate(
        [keys.reshape(rows, n_head, HEAD_DIM), values.reshape(rows, n_head, HEAD_DIM)], axis=2
    )
    own = lax.all_to_all(jnp.transpose(both, (1, 0, 2)), "head", split_axis=0, concat_axis=0, tiled=True)
    own = own.reshape(n_head * rows, 2 * HEAD_DIM)

    per = rows // n_blk
    q_out = jnp.transpose(query.reshape(n_blk, per, n_head, GROUP * HEAD_DIM), (0, 2, 1, 3))
    place = lax.dynamic_index_in_dim(positions, lax.div(head, quarters) * SEGLEN, 0, keepdims=False)
    place = lax.div(place, SEGLEN).astype(bf16)
    tag = jnp.full((n_blk, n_head, per, 128), place, bf16)
    q_out = jnp.concatenate([q_out, tag], axis=3).reshape(n_blk * n_head, per, GROUP * HEAD_DIM + 128)
    q_in = lax.all_to_all(q_out, ("blk", "head"), split_axis=0, concat_axis=0, tiled=True)
    order = q_in[::quarters, 0, GROUP * HEAD_DIM].astype(i32)
    q_in = q_in.reshape(n_blk * n_head * per, GROUP * HEAD_DIM + 128)

    half = n_head * rows
    near = jnp.concatenate([own, moved(own, 0, 1, 0)], axis=0)
    near_core = moved(near, 0, 0, 1)
    up, down = moved(near, 1, 0, 0), moved(near, -1, 0, 0)
    up_core, down_core = moved(up, 0, 0, 1), moved(down, 0, 0, 1)
    far_up, far_down = moved(up[:half], 1, 0, 0), moved(down[half:], -1, 0, 0)
    far_up_core, far_down_core = moved(far_up, 0, 0, 1), moved(far_down, 0, 0, 1)

    def of(dy, dx, dcore):
        return lax.rem(blk + 4 * dy + n_blk, n_blk) ^ (2 * dx + dcore)

    stacked, state = attention_call(
        order, blk, [of(0, 0, 0), of(0, 1, 0), of(0, 0, 1), of(0, 1, 1)], q_in, None, [near, near_core], False
    )
    state = attention_call(
        order,
        blk,
        [of(-1, 0, 0), of(-1, 1, 0), of(1, 0, 0), of(1, 1, 0), of(-1, 0, 1), of(-1, 1, 1), of(1, 0, 1), of(1, 1, 1)],
        stacked,
        state,
        [up, down, up_core, down_core],
        False,
    )
    out = attention_call(
        order,
        blk,
        [of(2, 0, 0), of(2, 1, 0), of(2, 0, 1), of(2, 1, 1)],
        stacked,
        state,
        [far_up, far_down, far_up_core, far_down_core],
        True,
    )
    out = out.reshape(n_blk * n_head, per, GROUP * HEAD_DIM)
    back = lax.all_to_all(out, ("blk", "head"), split_axis=0, concat_axis=0, tiled=True)
    back = back.reshape(n_blk, n_head, per, GROUP * HEAD_DIM)
    return jnp.transpose(back, (0, 2, 1, 3)).reshape(rows, HEADS * HEAD_DIM)


def solution(mesh):
    placed = (
        P(("blk", "head"), None),
        P(("blk", "head"), None),
        P(("blk", "head"), None),
        P("blk"),
    )
    return jax.shard_map(
        per_device, mesh=mesh, in_specs=placed, out_specs=P(("blk", "head"), None), check_vma=False
    )
```

time: 570 us -> 185 us (0.32)
  matrix products: 336 us -> 0 us
  Pallas kernels: 0 us -> 77.4 us
  other arithmetic: 71.2 us -> 1.47 us
  waiting for transfers between devices: 64.3 us -> 18 us
  starting transfers between devices: 3.6 us -> 35.5 us
  blocking collectives: 69.8 us -> 40 us
  between operations: 13.5 us -> 2.11 us
    dot_general x32 -> x0, matrix products: 336 us -> none  [the longest x16 203 us: update(): jnp.einsum('kgrs,skd->rkgd', weights.astype(jnp.bfloat16), v_tile, prefer...]
    pallas_call x0 -> x3, Pallas kernels: none -> 77.4 us  [attention_call(): pl.pallas_call(functools.partial(attend, sizes, first, last), out_shape=o...]
    all_gather x2 -> x0, waiting for transfers between devices: 64.2 us -> none  [the longest x1 55.6 us: per_device(): lax.all_gather(v_here, 'blk', axis=0, tiled=True)]
    reduce_sum x16 -> x0, other arithmetic: 58.1 us -> none  [update(): new_total = total * factor + jnp.sum(weights, axis=-1)]
    all_gather x1 -> x0, blocking collectives: 30.2 us -> none  [per_device(): lax.all_gather(positions, 'blk', axis=0, tiled=True)]
    ppermute x0 -> x10, starting transfers between devices: none -> 25.9 us  [moved(): return lax.ppermute(x, 'blk', pairs)]
    ppermute x0 -> x10, waiting for transfers between devices: none -> 16.1 us  [moved(): return lax.ppermute(x, 'blk', pairs)]
    le x16 -> x0, other arithmetic: 10.4 us -> none  [update(): visible = k_pos[None, :] <= q_pos[:, None]]
  transfers between devices with their start and end apart: 3 -> 11, of which waited for: 2 -> 3; matrix products, arithmetic and copies ran while one was open for 1% -> 3% of each run, Pallas kernels for 0% -> 32%
where the time goes in v1:
time: 185 us
  Pallas kernels  77.4 us (42%)
  blocking collectives  40 us (22%)
  starting transfers between devices  35.5 us (19%)
  waiting for transfers between devices  18 us (10%)
  local copies, waits for them, and re-layouts  9.98 us (5%)
  between operations  2.11 us (1%)
    pallas_call x3, Pallas kernels, attention_call(): pl.pallas_call(functools.partial(attend, sizes, first, last), out_shape=o...  77.4 us
    ppermute x10, starting transfers between devices, moved(): return lax.ppermute(x, 'blk', pairs)  25.9 us
    all_to_all x1, blocking collectives, per_device(): lax.all_to_all(out, ('blk', 'head'), split_axis=0, concat_axis=0, tiled=T...  24.7 us
    ppermute x10, waiting for transfers between devices, moved(): return lax.ppermute(x, 'blk', pairs)  16.1 us
    all_to_all x1, blocking collectives, per_device(): lax.all_to_all(jnp.transpose(both, (1, 0, 2)), 'head', split_axis=0, conc...  15.3 us
    all_to_all x1, starting transfers between devices, per_device(): lax.all_to_all(q_out, ('blk', 'head'), split_axis=0, concat_axis=0, tiled...  9.65 us
    unnamed x7, local copies, waits for them, and re-layouts  5.87 us
  transfers between devices with their start and end apart: 11, of which 3 were waited for; matrix products, arithmetic and copies ran while one was open for 3% of the time, Pallas kernels for 32%

profile of v1, /device:TPU:1, one launch (start us, length us, event | category | flops | bytes accessed | tf_op | source)
XLA Modules:
  0.0 184.6 jit_solution(6749170346692980848)
XLA Ops:
  0.0 1.1 copy.32
  1.1 1.1 copy.31
  2.5 15.3 %all_to_all.15 = bf16[8,128,256]{2,1,0:T(8,128)(2,1)S(1)} all-to-all(bf16[8,128,256]{2,1,0:T(8,128)(2,1)S(1)} %copy.33), channel_id=1, replica_groups=mesh['blk'=16,'head'=8] {'head'}, dimensions={0} | all-to-all | bytes 1048576 | tf_op jit(solution)/shard_map/all_to_all | solution.py:255
  17.9 2.5 %collective-permute-start = (bf16[1024,256]{1,0:T(8,128)(2,1)S(1)}, bf16[1024,256]{1,0:T(8,128)(2,1)S(1)}, u32[]{:S(2)}, u32[]{:S(2)}) collective-permute-start(bf16[1024,256]{1,0:T(8,128)(2,1)S(1)} %bitcast.101), channel_id=1, source_target_pairs={{0,16},{8,24},{16,0},{24,8},{32,48},{40,56},{48,32},{56,40},{64,80... | collective-permute-start | bytes 1572872 | tf_op jit(solution)/shard_map/ppermute | solution.py:243
  20.3 10.1 %collective-permute-done = bf16[1024,256]{1,0:T(8,128)(2,1)S(1)} collective-permute-done((bf16[1024,256]{1,0:T(8,128)(2,1)S(1)}, bf16[1024,256]{1,0:T(8,128)(2,1)S(1)}, u32[]{:S(2)}, u32[]{:S(2)}) %collective-permute-start) | collective-permute-done | bytes 524320 | tf_op jit(solution)/shard_map/ppermute | solution.py:243
  30.5 1.4 collective-permute-start.2
  31.8 1.5 collective-permute-start.3
  33.3 1.3 dynamic_slice.4
  36.6 1.2 concatenate.18
  37.8 9.6 %all-to-all-start = ((bf16[128,8,640]{2,1,0:T(8,128)(2,1)}), bf16[128,8,640]{2,1,0:T(8,128)(2,1)S(1)}, u32[]{:S(2)}, u32[]{:S(2)}) async-start(bf16[128,8,640]{2,1,0:T(8,128)(2,1)} %bitcast.99), calls=%async_computation | async-start | bytes 2621440 | tf_op jit(solution)/shard_map/all_to_all | solution.py:264
  47.6 1.1 collective-permute-start.1
  49.2 6.0 %collective-permute-done.2 = bf16[2048,256]{1,0:T(8,128)(2,1)S(1)} collective-permute-done((bf16[2048,256]{1,0:T(8,128)(2,1)S(1)}, bf16[2048,256]{1,0:T(8,128)(2,1)S(1)}, u32[]{:S(2)}, u32[]{:S(2)}) %collective-permute-start.2) | collective-permute-done | bytes 1048608 | tf_op jit(solution)/shard_map/ppermute | solution.py:243
  55.3 14.4 %collective-permute-start.4 = (bf16[2048,256]{1,0:T(8,128)(2,1)S(1)}, bf16[2048,256]{1,0:T(8,128)(2,1)}, u32[]{:S(2)}, u32[]{:S(2)}) collective-permute-start(bf16[2048,256]{1,0:T(8,128)(2,1)S(1)} %collective-permute-done.2), channel_id=1, source_target_pairs={{0,8},{8,0},{16,24},{24,16},{32,40},{40,32},{48,56},{56,48},{64,72... | collective-permute-start | bytes 3145736 | tf_op jit(solution)/shard_map/ppermute | solution.py:243
  70.0 1.9 %all-to-all-done = bf16[128,8,640]{2,1,0:T(8,128)(2,1)S(1)} async-done(((bf16[128,8,640]{2,1,0:T(8,128)(2,1)}), bf16[128,8,640]{2,1,0:T(8,128)(2,1)S(1)}, u32[]{:S(2)}, u32[]{:S(2)}) %all-to-all-start) | async-done | bytes 1310752 | tf_op jit(solution)/shard_map/all_to_all | solution.py:264
  72.7 0.9 collective-permute-start.6
  73.5 1.1 slice.13
  74.6 1.9 %collective-permute-start.7 = (bf16[1024,256]{1,0:T(8,128)(2,1)S(1)}, bf16[1024,256]{1,0:T(8,128)(2,1)S(1)}, u32[]{:S(2)}, u32[]{:S(2)}) collective-permute-start(bf16[1024,256]{1,0:T(8,128)(2,1)S(1)} %slice.13), channel_id=1, source_target_pairs={{0,96},{8,104},{16,112},{24,120},{32,0},{40,8},{48,16},{56,24},{64... | collective-permute-start | bytes 1572872 | tf_op jit(solution)/shard_map/ppermute | solution.py:243
  76.6 21.4 %shard_map.46 = (bf16[4608,128]{1,0:T(8,128)(2,1)S(1)}, f32[3,4096,128]{2,1,0:T(8,128)S(1)}) custom-call(s32[72]{0:T(128)S(1)} %get-tuple-element.10.refs_0_, bf16[1024,640]{1,0:T(8,128)(2,1)S(1)} %bitcast.91, bf16[4,512,256]{2,1,0:T(8,128)(2,1)S(1)} %bitcast.92, bf16[4,512,256]{2,1,0:T(8,128)(2,1)} %bitcast.34.refs_3_), custom_call_target="tpu_custom_call" | custom-call | flops 5368709120 | bytes 14680064 | tf_op jit(solution)/shard_map/pallas_call | solution.py:208
  98.0 2.7 %copy-done = f32[3,4096,128]{2,1,0:T(8,128)} copy-done((f32[3,4096,128]{2,1,0:T(8,128)}, f32[3,4096,128]{2,1,0:T(8,128)S(1)}, u32[]{:S(2)}) %copy-start) | copy-done | bytes 6291480
  100.7 1.9 %collective-permute-start.8 = (bf16[1024,256]{1,0:T(8,128)(2,1)S(1)}, bf16[1024,256]{1,0:T(8,128)(2,1)S(1)}, u32[]{:S(2)}, u32[]{:S(2)}) collective-permute-start(bf16[1024,256]{1,0:T(8,128)(2,1)S(1)} %collective-permute-done.6), channel_id=1, source_target_pairs={{0,8},{8,0},{16,24},{24,16},{32,40},{40,32},{48,56},{56,48},{64,72... | collective-permute-start | bytes 1572872 | tf_op jit(solution)/shard_map/ppermute | solution.py:243
  102.8 37.4 %shard_map.47.refs_2_ = f32[3,4096,128]{2,1,0:T(8,128)S(1)} custom-call(s32[72]{0:T(128)S(1)} %get-tuple-element.9.refs_0_, bf16[4608,128]{1,0:T(8,128)(2,1)S(1)} %get-tuple-element.7.refs_1_, f32[3,4096,128]{2,1,0:T(8,128)} %copy-done, bf16[4,512,256]{2,1,0:T(8,128)(2,1)S(1)} %bitcast.94, bf16[4,512,256]{2,1,0:T(8,128)(2,1)} %bitcast.60.refs_4_, ...), custom_call_target="tpu_custom_call" | custom-call | flops 10737418240 | bytes 16777216 | tf_op jit(solution)/shard_map/pallas_call | solution.py:208
  140.2 18.7 %shard_map.48 = bf16[1024,512]{1,0:T(8,128)(2,1)S(1)} custom-call(s32[72]{0:T(128)S(1)} %get-tuple-element.11.refs_0_, bf16[4608,128]{1,0:T(8,128)(2,1)S(1)} %get-tuple-element.7.refs_1_, f32[3,4096,128]{2,1,0:T(8,128)S(1)} %shard_map.47.refs_2_, bf16[2,512,256]{2,1,0:T(8,128)(2,1)S(1)} %bitcast.95, bf16[2,512,256]{2,1,0:T(8,128)(2,1)S(1)} %bitcast.96, ...), custom_call_target="tpu_custom_call" | custom-call | flops 5368709120 | bytes 14680064 | tf_op jit(solution)/shard_map/pallas_call | solution.py:208
  158.9 24.7 %all_to_all.16 = bf16[128,8,512]{2,1,0:T(8,128)(2,1)S(1)} all-to-all(bf16[128,8,512]{2,1,0:T(8,128)(2,1)S(1)} %bitcast.93), channel_id=1, replica_groups=mesh['blk'=16,'head'=8] {'blk','head'}, dimensions={0} | all-to-all | bytes 2097152 | tf_op jit(solution)/shard_map/all_to_all | solution.py:301
  183.6 1.0 copy.35
  (34 shorter events, 2.4 us)
Async XLA Ops:
  2.3 34.3 %copy-start.1 = (bf16[128,4096]{1,0:T(8,128)(2,1)S(1)}, bf16[128,4096]{1,0:T(8,128)(2,1)}, u32[]{:S(2)}) copy-start(bf16[128,4096]{1,0:T(8,128)(2,1)} %param.4) | copy-start | bytes 3145732
  17.9 12.5 %collective-permute-start = (bf16[1024,256]{1,0:T(8,128)(2,1)S(1)}, bf16[1024,256]{1,0:T(8,128)(2,1)S(1)}, u32[]{:S(2)}, u32[]{:S(2)}) collective-permute-start(bf16[1024,256]{1,0:T(8,128)(2,1)S(1)} %bitcast.101), channel_id=1, source_target_pairs={{0,16},{8,24},{16,0},{24,8},{32,48},{40,56},{48,32},{56,40},{64,80... | collective-permute-start | bytes 1572872 | tf_op jit(solution)/shard_map/ppermute | solution.py:243
  30.5 24.8 %collective-permute-start.2 = (bf16[2048,256]{1,0:T(8,128)(2,1)S(1)}, bf16[2048,256]{1,0:T(8,128)(2,1)S(1)}, u32[]{:S(2)}, u32[]{:S(2)}) collective-permute-start(bf16[2048,256]{1,0:T(8,128)(2,1)S(1)} %pad_maximum_fusion), channel_id=1, source_target_pairs={{0,32},{8,40},{16,48},{24,56},{32,64},{40,72},{48,80},{56,88},{64,... | collective-permute-start | bytes 3145736 | tf_op jit(solution)/shard_map/ppermute | solution.py:243
  31.8 37.8 %collective-permute-start.3 = (bf16[2048,256]{1,0:T(8,128)(2,1)S(1)}, bf16[2048,256]{1,0:T(8,128)(2,1)}, u32[]{:S(2)}, u32[]{:S(2)}) collective-permute-start(bf16[2048,256]{1,0:T(8,128)(2,1)S(1)} %pad_maximum_fusion), channel_id=1, source_target_pairs={{0,96},{8,104},{16,112},{24,120},{32,0},{40,8},{48,16},{56,24},{64... | collective-permute-start | bytes 3145736 | tf_op jit(solution)/shard_map/ppermute | solution.py:243
  37.8 34.1 %all-to-all-start = ((bf16[128,8,640]{2,1,0:T(8,128)(2,1)}), bf16[128,8,640]{2,1,0:T(8,128)(2,1)S(1)}, u32[]{:S(2)}, u32[]{:S(2)}) async-start(bf16[128,8,640]{2,1,0:T(8,128)(2,1)} %bitcast.99), calls=%async_computation | async-start | bytes 2621440 | tf_op jit(solution)/shard_map/all_to_all | solution.py:264
  47.6 29.0 %collective-permute-start.1 = (bf16[2048,256]{1,0:T(8,128)(2,1)S(1)}, bf16[2048,256]{1,0:T(8,128)(2,1)}, u32[]{:S(2)}, u32[]{:S(2)}) collective-permute-start(bf16[2048,256]{1,0:T(8,128)(2,1)S(1)} %pad_maximum_fusion), channel_id=1, source_target_pairs={{0,8},{8,0},{16,24},{24,16},{32,40},{40,32},{48,56},{56,48},{64,72... | collective-permute-start | bytes 3145736 | tf_op jit(solution)/shard_map/ppermute | solution.py:243
  55.3 47.5 %collective-permute-start.4 = (bf16[2048,256]{1,0:T(8,128)(2,1)S(1)}, bf16[2048,256]{1,0:T(8,128)(2,1)}, u32[]{:S(2)}, u32[]{:S(2)}) collective-permute-start(bf16[2048,256]{1,0:T(8,128)(2,1)S(1)} %collective-permute-done.2), channel_id=1, source_target_pairs={{0,8},{8,0},{16,24},{24,16},{32,40},{40,32},{48,56},{56,48},{64,72... | collective-permute-start | bytes 3145736 | tf_op jit(solution)/shard_map/ppermute | solution.py:243
  69.7 33.1 %collective-permute-start.5 = (bf16[2048,256]{1,0:T(8,128)(2,1)}, bf16[2048,256]{1,0:T(8,128)(2,1)}, u32[]{:S(2)}, u32[]{:S(2)}) collective-permute-start(bf16[2048,256]{1,0:T(8,128)(2,1)} %collective-permute-done.3), channel_id=1, source_target_pairs={{0,8},{8,0},{16,24},{24,16},{32,40},{40,32},{48,56},{56,48},{64,72... | collective-permute-start | bytes 3145736 | tf_op jit(solution)/shard_map/ppermute | solution.py:243
  72.7 28.0 %collective-permute-start.6 = (bf16[1024,256]{1,0:T(8,128)(2,1)S(1)}, bf16[1024,256]{1,0:T(8,128)(2,1)S(1)}, u32[]{:S(2)}, u32[]{:S(2)}) collective-permute-start(bf16[1024,256]{1,0:T(8,128)(2,1)S(1)} %slice.12), channel_id=1, source_target_pairs={{0,32},{8,40},{16,48},{24,56},{32,64},{40,72},{48,80},{56,88},{64,... | collective-permute-start | bytes 1572872 | tf_op jit(solution)/shard_map/ppermute | solution.py:243
  74.6 27.9 %collective-permute-start.7 = (bf16[1024,256]{1,0:T(8,128)(2,1)S(1)}, bf16[1024,256]{1,0:T(8,128)(2,1)S(1)}, u32[]{:S(2)}, u32[]{:S(2)}) collective-permute-start(bf16[1024,256]{1,0:T(8,128)(2,1)S(1)} %slice.13), channel_id=1, source_target_pairs={{0,96},{8,104},{16,112},{24,120},{32,0},{40,8},{48,16},{56,24},{64... | collective-permute-start | bytes 1572872 | tf_op jit(solution)/shard_map/ppermute | solution.py:243
  98.0 2.7 %copy-start = (f32[3,4096,128]{2,1,0:T(8,128)}, f32[3,4096,128]{2,1,0:T(8,128)S(1)}, u32[]{:S(2)}) copy-start(f32[3,4096,128]{2,1,0:T(8,128)S(1)} %get-tuple-element.8.refs_2_) | copy-start | bytes 18874372
  100.7 39.5 %collective-permute-start.8 = (bf16[1024,256]{1,0:T(8,128)(2,1)S(1)}, bf16[1024,256]{1,0:T(8,128)(2,1)S(1)}, u32[]{:S(2)}, u32[]{:S(2)}) collective-permute-start(bf16[1024,256]{1,0:T(8,128)(2,1)S(1)} %collective-permute-done.6), channel_id=1, source_target_pairs={{0,8},{8,0},{16,24},{24,16},{32,40},{40,32},{48,56},{56,48},{64,72... | collective-permute-start | bytes 1572872 | tf_op jit(solution)/shard_map/ppermute | solution.py:243
  102.5 37.7 %collective-permute-start.9 = (bf16[1024,256]{1,0:T(8,128)(2,1)S(1)}, bf16[1024,256]{1,0:T(8,128)(2,1)S(1)}, u32[]{:S(2)}, u32[]{:S(2)}) collective-permute-start(bf16[1024,256]{1,0:T(8,128)(2,1)S(1)} %collective-permute-done.7), channel_id=1, source_target_pairs={{0,8},{8,0},{16,24},{24,16},{32,40},{40,32},{48,56},{56,48},{64,72... | collective-permute-start | bytes 1572872 | tf_op jit(solution)/shard_map/ppermute | solution.py:243

commit v2 on v0

v2 whole, which is shorter than its diff:
```python
import functools

import jax
import jax.numpy as jnp
import numpy as np
from jax import lax
from jax.experimental import pallas as pl
from jax.experimental.pallas import tpu as pltpu
from jax.sharding import PartitionSpec as P

HEADS = 32
KV_HEADS = 8
HEAD_DIM = 128
GROUP = HEADS // KV_HEADS
SEGLEN = 512
SEGS = 32
PART = SEGLEN // 16
TILE = GROUP * PART
ROWS = SEGS * TILE
QSEGS = 4
QB = QSEGS * TILE
BLOCKS = SEGS // QSEGS
UNROLL = 4
WIDE = 2 * HEAD_DIM
LOG2E = 1.4426950408889634
SCALE = HEAD_DIM**-0.5 * LOG2E
SAFE = 48.0
LOW = -1e30
NT = (((1,), (1,)), ((), ()))
bf16, f32, i32 = jnp.bfloat16, jnp.float32, jnp.int32

STEPS = [(b, b) for b in range(BLOCKS)] + [(q, k) for k in range(BLOCKS) for q in range(k + 1, BLOCKS)]


def attend(n, done, first, last, *refs):
    refs = list(refs)
    meta, q_ref = refs[:2]
    refs = refs[2:]
    if not first:
        acc_in, m_in = refs[:2]
        refs = refs[2:]
    chunks, refs = refs[:n], refs[n:]
    qs = refs.pop(0) if first else q_ref
    acc, m_out = refs[:2]
    refs = refs[2:]
    if last:
        out = refs.pop(0)
    kv, m_ref, s_scr, p_scr, q_pos, k_pos, m_sem = refs
    shifted = meta[SEGS]
    part = n * PART
    keys = QSEGS * part

    row = lax.broadcasted_iota(i32, (QB, 128), 0)
    place = lax.rem(row, PART)
    q_pos[...] = lax.div(row, TILE) * SEGLEN + lax.div(place, 8) * 128 + lax.rem(place, 8) + meta[SEGS + 1]
    column = lax.broadcasted_iota(i32, (8, keys), 1)
    within = sum(jnp.where(column >= i * part, 1, 0) for i in range(1, QSEGS))
    chunk = column - within * part
    offset = sum(jnp.where(lax.div(chunk, PART) == c, meta[SEGS + 8 + 2 * len(STEPS) + done + c], 0) for c in range(n))
    place = lax.rem(chunk, PART)
    k_pos[...] = within * SEGLEN + lax.div(place, 8) * 128 + lax.rem(place, 8) + offset
    kv[:, :, WIDE:] = jnp.ones((BLOCKS, keys, HEAD_DIM), bf16)

    def lay(s, _):
        p = meta[s]
        block, within = lax.div(p, QSEGS), lax.rem(p, QSEGS)
        rows = pl.ds(pl.multiple_of(s * PART, PART), PART)
        for c in range(n):
            to = pl.ds(pl.multiple_of(within * part + c * PART, PART), PART)
            kv[block, to, :WIDE] = chunks[c][rows, :]
        if first:
            for g in range(GROUP):
                to = pl.ds(pl.multiple_of(p * TILE + g * PART, PART), PART)
                qs[to, :] = q_ref[rows, g * HEAD_DIM : (g + 1) * HEAD_DIM]
        return 0

    lax.fori_loop(0, SEGS, lay, 0)

    def step_of(t):
        if isinstance(t, int):
            return STEPS[t]
        return meta[SEGS + 8 + t], meta[SEGS + 8 + len(STEPS) + t]

    def rows_of(block):
        return pl.ds(pl.multiple_of(block * QB, QB), QB)

    def scores(t):
        q_block, k_block = step_of(t)
        return lax.dot_general(
            qs[rows_of(q_block), :], kv[k_block, :, :HEAD_DIM], NT, preferred_element_type=f32
        )

    def seen(c):
        return k_pos[0:1, c : c + 128] <= q_pos[...]

    def weigh(t, slot, masked):
        weights = jnp.exp2(scores(t) * SCALE)
        if masked:
            for c in range(0, keys, 128):
                kept = jnp.where(seen(c), weights[:, c : c + 128], 0.0)
                p_scr[slot, :, c : c + 128] = kept.astype(bf16)
        else:
            p_scr[slot] = weights.astype(bf16)

    def collect(t, slot):
        return jnp.dot(p_scr[slot], kv[step_of(t)[1], :, HEAD_DIM:], preferred_element_type=f32)

    @pl.when(shifted == 0)
    def _():
        for t in range(BLOCKS):
            weigh(t, t % 2, True)
            if t:
                rows = rows_of(t - 1)
                added = collect(t - 1, (t - 1) % 2)
                acc[rows, :] = added if first else acc_in[rows, :] + added

        rows, added = rows_of(BLOCKS - 1), collect(BLOCKS - 1, (BLOCKS - 1) % 2)
        acc[rows, :] = added if first else acc_in[rows, :] + added
        weigh(BLOCKS, 0, False)

        def body(u, _):
            for r in range(UNROLL):
                t = BLOCKS + u * UNROLL + r
                weigh(jnp.minimum(t + 1, len(STEPS) - 1), (r + 1) % 2, False)
                acc[rows_of(step_of(t)[0]), :] += collect(t, r % 2)
            return 0

        assert (len(STEPS) - BLOCKS) % UNROLL == 0
        lax.fori_loop(0, (len(STEPS) - BLOCKS) // UNROLL, body, 0)

    @pl.when(shifted != 0)
    def _():
        if first:
            m_ref[...] = jnp.full_like(m_ref, LOW)
            acc[...] = jnp.zeros_like(acc)
        else:
            copy = pltpu.make_async_copy(m_in, m_ref, m_sem)
            copy.start()
            copy.wait()
            acc[...] = acc_in[...]

        def step(masked):
            def body(t, _):
                rows = rows_of(step_of(t)[0])
                s_scr[...] = scores(t) * SCALE
                if masked:
                    for c in range(0, keys, 128):
                        s_scr[:, c : c + 128] = jnp.where(seen(c), s_scr[:, c : c + 128], LOW)
                before = m_ref[rows, :]
                now = jnp.maximum(before, jnp.max(s_scr[...], axis=1, keepdims=True))
                factor = jnp.exp2(before - now)
                m_ref[rows, :] = now
                for c in range(0, keys, 128):
                    p_scr[0, :, c : c + 128] = jnp.exp2(s_scr[:, c : c + 128] - now).astype(bf16)
                added = collect(t, 0)
                for c in (0, HEAD_DIM):
                    to = slice(c, c + HEAD_DIM)
                    acc[rows, to] = acc[rows, to] * factor + added[:, to]
                return 0

            return body

        lax.fori_loop(0, BLOCKS, step(True), 0)
        lax.fori_loop(BLOCKS, len(STEPS), step(False), 0)
        copy = pltpu.make_async_copy(m_ref, m_out, m_sem)
        copy.start()
        copy.wait()

    if last:
        def finish(s, _):
            p = meta[s]
            for g in range(GROUP):
                rows = pl.ds(pl.multiple_of(p * TILE + g * PART, PART), PART)
                out[pl.ds(pl.multiple_of(s * PART, PART), PART), g * HEAD_DIM : (g + 1) * HEAD_DIM] = (
                    acc[rows, :HEAD_DIM] / acc[rows, HEAD_DIM:]
                ).astype(bf16)
            return 0

        lax.fori_loop(0, SEGS, finish, 0)


def attention_call(meta, done, q, state, chunks, last):
    first, n = state is None, len(chunks)
    keys = QSEGS * n * PART
    vmem, hbm = pl.BlockSpec(memory_space=pltpu.VMEM), pl.BlockSpec(memory_space=pl.ANY)
    smem = pl.BlockSpec(memory_space=pltpu.SMEM)
    operands = [meta, q] + ([] if first else list(state)) + chunks
    in_specs = [smem, vmem] + ([] if first else [vmem, hbm]) + [vmem] * n
    out_shape = [jax.ShapeDtypeStruct((ROWS, WIDE), f32), jax.ShapeDtypeStruct((ROWS, 128), f32)]
    out_specs = [vmem, hbm]
    if first:
        out_shape = [jax.ShapeDtypeStruct((ROWS, HEAD_DIM), bf16)] + out_shape
        out_specs = [vmem] + out_specs
    if last:
        out_shape = out_shape + [jax.ShapeDtypeStruct((SEGS * PART, GROUP * HEAD_DIM), bf16)]
        out_specs = out_specs + [vmem]
    return pl.pallas_call(
        functools.partial(attend, n, done, first, last),
        out_shape=tuple(out_shape),
        in_specs=in_specs,
        out_specs=tuple(out_specs),
        input_output_aliases={} if first else {2: 0},
        scratch_shapes=[
            pltpu.VMEM((BLOCKS, keys, WIDE + HEAD_DIM), bf16),
            pltpu.VMEM((ROWS, 128), f32),
            pltpu.VMEM((QB, keys), f32),
            pltpu.VMEM((2, QB, keys), bf16),
            pltpu.VMEM((QB, 128), i32),
            pltpu.VMEM((8, keys), i32),
            pltpu.SemaphoreType.DMA,
        ],
        compiler_params=pltpu.CompilerParams(vmem_limit_bytes=36 * 2**20),
        cost_estimate=pl.CostEstimate(
            flops=len(STEPS) * QB * keys * 4 * WIDE,
            bytes_accessed=n * SEGS * PART * 512 + ROWS * WIDE * 4,
            transcendentals=len(STEPS) * QB * keys,
        ),
    )(*operands)


def held(step, *arrays):
    hbm = pl.BlockSpec(memory_space=pl.ANY)

    def nothing(*refs):
        del refs

    return pl.pallas_call(
        nothing,
        out_shape=tuple(jax.ShapeDtypeStruct(a.shape, a.dtype) for a in arrays),
        in_specs=[hbm] * (1 + len(arrays)),
        out_specs=(hbm,) * len(arrays),
        input_output_aliases={1 + i: i for i in range(len(arrays))},
        compiler_params=pltpu.CompilerParams(vmem_limit_bytes=2**20),
    )(step, *arrays)


def moved(x, dy, dx, dcore):
    pairs = []
    for y in range(4):
        for x_hi in range(2):
            for core in range(2):
                to = ((y + dy) % 4) * 4 + (x_hi ^ dx) * 2 + (core ^ dcore)
                pairs.append((y * 4 + x_hi * 2 + core, to))
    return lax.ppermute(x, "blk", pairs)


def per_device(query, keys, values, positions):
    n_blk, n_head = lax.axis_size("blk"), lax.axis_size("head")
    blk, head = lax.axis_index("blk"), lax.axis_index("head")
    rows = query.shape[0]
    quarters = SEGLEN // rows

    per = rows // n_blk

    def spread(x):
        return jnp.transpose(x.reshape(n_blk, per, n_head, -1), (0, 2, 1, 3))

    def longest(x):
        heads = x.shape[1] // HEAD_DIM
        same = np.arange(x.shape[1])[:, None] // HEAD_DIM == np.arange(heads)
        squares = jnp.dot(x * x, jnp.asarray(same, bf16), preferred_element_type=f32)
        return jnp.max(squares.reshape(rows, n_head, -1), axis=(0, 2)) * 1.02

    place = jnp.where(head < quarters, positions[0], positions[SEGLEN])
    place = lax.div(place, SEGLEN).astype(f32)
    lane = lax.broadcasted_iota(i32, (n_head, 128), 1)
    tag = jnp.where(lane == 0, place, jnp.where(lane == 1, longest(query)[:, None], longest(keys)[:, None]))
    tag = jnp.broadcast_to(tag.astype(bf16)[None, :, None, :], (n_blk, n_head, per, 128))
    sent = jnp.concatenate([spread(query), spread(keys), spread(values), tag], axis=3)
    width = GROUP * HEAD_DIM
    sent = sent.reshape(n_blk * n_head, per, width + WIDE + 128)
    got = lax.all_to_all(sent, ("blk", "head"), split_axis=0, concat_axis=0, tiled=True)
    tags = got[:, 0, width + WIDE :].astype(f32)
    order = tags[::quarters, 0].astype(i32)
    most = jnp.max(tags[:, 1]) * jnp.max(tags[:, 2]) * (SCALE * SCALE)
    shifted = jnp.where(most <= SAFE * SAFE, 0, 1)
    listed = jnp.asarray([q for q, _ in STEPS] + [k for _, k in STEPS], i32)
    offsets = [(0, 0, 0), (0, 0, 1), (0, 1, 0), (0, 1, 1), (-1, 0, 0), (1, 0, 0)]
    offsets += [(-1, 0, 1), (1, 0, 1), (-1, 1, 0), (1, 1, 0)]
    offsets += [(-1, 1, 1), (1, 1, 1), (2, 0, 0), (2, 1, 0), (2, 0, 1), (2, 1, 1)]
    first_row = 8 * jnp.stack([lax.rem(blk + 4 * dy + n_blk, n_blk) ^ (2 * dx + dcore) for dy, dx, dcore in offsets])
    common = jnp.stack([shifted, blk * 8] + [jnp.zeros_like(blk)] * 6)
    meta = jnp.concatenate([order, common, listed, first_row])
    got = got.reshape(n_blk * n_head * per, width + WIDE + 128)
    own = got[:, width : width + WIDE]

    x, own_core = moved(own, 0, 1, 0), moved(own, 0, 0, 1)
    own_up, own_down = moved(own, 1, 0, 0), moved(own, -1, 0, 0)
    call = attention_call(meta, 0, got, None, [own, own_core], False)
    stacked, state = call[0], call[1:]

    x, own_up, own_down = held(state[1], x, own_up, own_down)
    x_up, x_down, x_core = moved(x, 1, 0, 0), moved(x, -1, 0, 0), moved(x, 0, 0, 1)
    own_up_core, own_down_core = moved(own_up, 0, 0, 1), moved(own_down, 0, 0, 1)
    state = attention_call(meta, 2, stacked, state, [x, x_core, own_up, own_down], False)

    x_up, x_down, own_up = held(state[1], x_up, x_down, own_up)
    own_far, x_far = moved(own_up, 1, 0, 0), moved(x_down, -1, 0, 0)
    x_up_core, x_down_core = moved(x_up, 0, 0, 1), moved(x_down, 0, 0, 1)
    state = attention_call(meta, 6, stacked, state, [own_up_core, own_down_core, x_up, x_down], False)

    own_far, x_far = held(state[1], own_far, x_far)
    own_far_core, x_far_core = moved(own_far, 0, 0, 1), moved(x_far, 0, 0, 1)
    chunks = [x_up_core, x_down_core, own_far, x_far, own_far_core, x_far_core]
    out = attention_call(meta, 10, stacked, state, chunks, True)[-1]
    out = out.reshape(n_blk * n_head, per, GROUP * HEAD_DIM)
    back = lax.all_to_all(out, ("blk", "head"), split_axis=0, concat_axis=0, tiled=True)
    back = back.reshape(n_blk, n_head, per, GROUP * HEAD_DIM)
    return jnp.transpose(back, (0, 2, 1, 3)).reshape(rows, HEADS * HEAD_DIM)


def solution(mesh):
    placed = (
        P(("blk", "head"), None),
        P(("blk", "head"), None),
        P(("blk", "head"), None),
        P("blk"),
    )
    return jax.shard_map(
        per_device, mesh=mesh, in_specs=placed, out_specs=P(("blk", "head"), None), check_vma=False
    )
```

time: 570 us -> 223 us (0.39)
  matrix products: 336 us -> 2.51 us
  Pallas kernels: 0 us -> 134 us
  other arithmetic: 71.2 us -> 2.61 us
  blocking collectives: 69.8 us -> 26 us
  waiting for transfers between devices: 64.3 us -> 29 us
  starting transfers between devices: 3.6 us -> 22.7 us
  between operations: 13.5 us -> 2.76 us
  local copies, waits for them, and re-layouts: 9.74 us -> 3.55 us
    dot_general x32 -> x2, matrix products: 336 us -> 2.51 us  [longest(): jnp.dot(x * x, jnp.asarray(same, bf16), preferred_element_type=f32)]
    pallas_call x0 -> x7, Pallas kernels: none -> 134 us  [the longest x4 134 us: attention_call(): pl.pallas_call(functools.partial(attend, n, done, first, last), out_shape...]
    all_gather x2 -> x0, waiting for transfers between devices: 64.2 us -> none  [the longest x1 55.6 us: per_device(): lax.all_gather(v_here, 'blk', axis=0, tiled=True)]
    reduce_sum x16 -> x0, other arithmetic: 58.1 us -> none  [update(): new_total = total * factor + jnp.sum(weights, axis=-1)]
    all_gather x1 -> x0, blocking collectives: 30.2 us -> none  [per_device(): lax.all_gather(positions, 'blk', axis=0, tiled=True)]
    all_to_all x1, waiting for transfers between devices: 0.01 us -> 26.8 us  [per_device(): lax.all_to_all(sent, ('blk', 'head'), split_axis=0, concat_axis=0, tiled=...]
    all_to_all x3 -> x1, blocking collectives: 39.6 us -> 26 us  [per_device(): lax.all_to_all(out, ('blk', 'head'), split_axis=0, concat_axis=0, tiled=T...]
    ppermute x0 -> x15, starting transfers between devices: none -> 11.2 us  [moved(): return lax.ppermute(x, 'blk', pairs)]
  transfers between devices with their start and end apart: 3 -> 16, of which waited for: 2 -> 3; matrix products, arithmetic and copies ran while one was open for 1% -> 0% of each run, Pallas kernels for 0% -> 39%
where the time goes in v2:
time: 223 us
  Pallas kernels  134 us (60%)
  waiting for transfers between devices  29 us (13%)
  blocking collectives  26 us (12%)
  starting transfers between devices  22.7 us (10%)
  local copies, waits for them, and re-layouts  3.55 us (2%)
  between operations  2.76 us (1%)
  other arithmetic  2.61 us (1%)
  matrix products  2.51 us (1%)
    pallas_call x4, Pallas kernels, attention_call(): pl.pallas_call(functools.partial(attend, n, done, first, last), out_shape...  134 us
    all_to_all x1, waiting for transfers between devices, per_device(): lax.all_to_all(sent, ('blk', 'head'), split_axis=0, concat_axis=0, tiled=...  26.8 us
    all_to_all x1, blocking collectives, per_device(): lax.all_to_all(out, ('blk', 'head'), split_axis=0, concat_axis=0, tiled=T...  26 us
    all_to_all x1, starting transfers between devices, per_device(): lax.all_to_all(sent, ('blk', 'head'), split_axis=0, concat_axis=0, tiled=...  11.5 us
    ppermute x15, starting transfers between devices, moved(): return lax.ppermute(x, 'blk', pairs)  11.2 us
  transfers between devices with their start and end apart: 16, of which 3 were waited for; matrix products, arithmetic and copies ran while one was open for 0% of the time, Pallas kernels for 39%

profile of v2, /device:TPU:1, one launch (start us, length us, event | category | flops | bytes accessed | tf_op | source)
XLA Modules:
  0.0 222.7 jit_solution(4885249671567016970)
XLA Ops:
  0.0 1.4 fusion.2
  2.7 2.2 convolution_reduce_fusion
  5.6 1.5 pad_maximum_fusion
  7.2 11.5 %all-to-all-start = ((bf16[128,8,896]{2,1,0:T(8,128)(2,1)}), bf16[128,8,896]{2,1,0:T(8,128)(2,1)S(1)}, u32[]{:S(2)}, u32[]{:S(2)}) async-start(bf16[128,8,896]{2,1,0:T(8,128)(2,1)} %bitcast.43), calls=%async_computation | async-start | bytes 3670016 | tf_op jit(solution)/shard_map/all_to_all | solution.py:272
  18.8 26.8 %all-to-all-done = bf16[128,8,896]{2,1,0:T(8,128)(2,1)S(1)} async-done(((bf16[128,8,896]{2,1,0:T(8,128)(2,1)}), bf16[128,8,896]{2,1,0:T(8,128)(2,1)S(1)}, u32[]{:S(2)}, u32[]{:S(2)}) %all-to-all-start) | async-done | bytes 1835040 | tf_op jit(solution)/shard_map/all_to_all | solution.py:272
  45.5 0.8 slice.31.refs_2_
  46.4 1.7 collective-permute-start
  48.1 0.8 collective-permute-start.3
  48.9 0.6 collective-permute-start.2
  49.6 0.6 collective-permute-start.1
  50.2 0.7 slice_reduce_fusion
  52.3 22.1 %shard_map.73 = (bf16[4096,128]{1,0:T(8,128)(2,1)S(1)}, f32[4096,256]{1,0:T(8,128)S(1)}, f32[4096,128]{1,0:T(8,128)S(1)}) custom-call(s32[128]{0:T(128)S(1)} %concatenate.7.refs_0_, bf16[1024,896]{1,0:T(8,128)(2,1)S(1)} %bitcast.41, bf16[1024,256]{1,0:T(8,128)(2,1)} %slice.31.refs_2_, bf16[1024,256]{1,0:T(8,128)(2,1)} %collective-permute-done.refs_3_), custom_call_target="tpu_custom_call" | custom-call | flops 4831838208 | bytes 5242880 | tf_op jit(solution)/shard_map/pallas_call | solution.py:197
  74.5 0.9 collective-permute-start.4
  75.4 1.7 collective-permute-start.8
  77.7 32.6 %shard_map.75 = (f32[4096,256]{1,0:T(8,128)S(1)}, f32[4096,128]{1,0:T(8,128)S(1)}) custom-call(s32[128]{0:T(128)S(1)} %concatenate.7.refs_0_, bf16[4096,128]{1,0:T(8,128)(2,1)S(1)} %get-tuple-element.21.refs_1_, f32[4096,256]{1,0:T(8,128)S(1)} %get-tuple-element.22.refs_2_, ...), custom_call_target="tpu_custom_call", output_to_operand_aliasing={{0}: (2, {})} | custom-call | flops 9663676416 | bytes 6291456 | tf_op jit(solution)/shard_map/pallas_call | solution.py:197
  110.3 2.9 %collective-permute-start.12 = (bf16[1024,256]{1,0:T(8,128)(2,1)S(1)}, bf16[1024,256]{1,0:T(8,128)(2,1)S(1)}, u32[]{:S(2)}, u32[]{:S(2)}) collective-permute-start(bf16[1024,256]{1,0:T(8,128)(2,1)S(1)} %get-tuple-element.30.refs_7_), channel_id=1, source_target_pairs={{0,96},{8,104},{16,112},{24,120},{32,0},{40,8},{48,16},{56,24},{64... | collective-permute-start | bytes 1572872 | tf_op jit(solution)/shard_map/ppermute | solution.py:244
  113.2 0.8 collective-permute-start.10
  114.0 32.7 %shard_map.77 = (f32[4096,256]{1,0:T(8,128)S(1)}, f32[4096,128]{1,0:T(8,128)S(1)}) custom-call(s32[128]{0:T(128)S(1)} %concatenate.7.refs_0_, bf16[4096,128]{1,0:T(8,128)(2,1)S(1)} %get-tuple-element.21.refs_1_, f32[4096,256]{1,0:T(8,128)S(1)} %get-tuple-element.27.refs_2_, ...), custom_call_target="tpu_custom_call", output_to_operand_aliasing={{0}: (2, {})} | custom-call | flops 9663676416 | bytes 6291456 | tf_op jit(solution)/shard_map/pallas_call | solution.py:197
  146.7 0.6 collective-permute-start.13
  147.4 1.4 collective-permute-done.13.refs_8_
  148.8 0.7 collective-permute-done.14.refs_9_
  149.6 46.2 %shard_map.79 = (f32[4096,256]{1,0:T(8,128)S(1)}, f32[4096,128]{1,0:T(8,128)}, bf16[1024,512]{1,0:T(8,128)(2,1)S(1)}) custom-call(s32[128]{0:T(128)S(1)} %concatenate.7.refs_0_, bf16[4096,128]{1,0:T(8,128)(2,1)S(1)} %get-tuple-element.21.refs_1_, f32[4096,256]{1,0:T(8,128)S(1)} %get-tuple-element.31.refs_2_, ...), custom_call_target="tpu_custom_call", output_to_operand_aliasing={{0}: (2, {})} | custom-call | flops 14495514624 | bytes 7340032 | tf_op jit(solution)/shard_map/pallas_call | solution.py:197
  195.8 26.0 %all_to_all.10 = bf16[128,8,512]{2,1,0:T(8,128)(2,1)S(1)} all-to-all(bf16[128,8,512]{2,1,0:T(8,128)(2,1)S(1)} %bitcast.42), channel_id=1, replica_groups=mesh['blk'=16,'head'=8] {'blk','head'}, dimensions={0} | all-to-all | bytes 2097152 | tf_op jit(solution)/shard_map/all_to_all | solution.py:307
  221.8 1.0 copy.33
  (47 shorter events, 1.7 us)
Async XLA Ops:
  0.0 5.0 %copy-start.3 = (bf16[1024,8]{1,0:T(8,128)(2,1)S(1)}, bf16[1024,8]{1,0:T(8,128)(2,1)}, u32[]{:S(2)}) copy-start(bf16[1024,8]{1,0:T(8,128)(2,1)} %constant.63.clone) | copy-start | bytes 49156
  0.0 5.6 %copy-start = (bf16[128,4096]{1,0:T(8,128)(2,1)S(1)}, bf16[128,4096]{1,0:T(8,128)(2,1)}, u32[]{:S(2)}) copy-start(bf16[128,4096]{1,0:T(8,128)(2,1)} %param.7) | copy-start | bytes 3145732
  0.0 5.0 %copy-start.1 = (bf16[128,1024]{1,0:T(8,128)(2,1)S(1)}, bf16[128,1024]{1,0:T(8,128)(2,1)}, u32[]{:S(2)}) copy-start(bf16[128,1024]{1,0:T(8,128)(2,1)} %param.8) | copy-start | bytes 786436
  0.0 5.6 %copy-start.2 = (bf16[128,1024]{1,0:T(8,128)(2,1)S(1)}, bf16[128,1024]{1,0:T(8,128)(2,1)}, u32[]{:S(2)}) copy-start(bf16[128,1024]{1,0:T(8,128)(2,1)} %param.9) | copy-start | bytes 786436
  7.2 45.1 %copy-start.4 = (s32[72]{0:T(128)S(1)}, s32[72]{0:T(128)}, u32[]{:S(2)}) copy-start(s32[72]{0:T(128)} %constant.64.clone) | copy-start | bytes 868
  7.2 38.4 %all-to-all-start = ((bf16[128,8,896]{2,1,0:T(8,128)(2,1)}), bf16[128,8,896]{2,1,0:T(8,128)(2,1)S(1)}, u32[]{:S(2)}, u32[]{:S(2)}) async-start(bf16[128,8,896]{2,1,0:T(8,128)(2,1)} %bitcast.43), calls=%async_computation | async-start | bytes 3670016 | tf_op jit(solution)/shard_map/all_to_all | solution.py:272
  46.4 6.0 %collective-permute-start = (bf16[1024,256]{1,0:T(8,128)(2,1)}, bf16[1024,256]{1,0:T(8,128)(2,1)}, u32[]{:S(2)}, u32[]{:S(2)}) collective-permute-start(bf16[1024,256]{1,0:T(8,128)(2,1)} %slice.31.refs_2_), channel_id=1, source_target_pairs={{0,8},{8,0},{16,24},{24,16},{32,40},{40,32},{48,56},{56,48},{64,72... | collective-permute-start | bytes 1572872 | tf_op jit(solution)/shard_map/ppermute | solution.py:244
  48.1 26.4 %collective-permute-start.3 = (bf16[1024,256]{1,0:T(8,128)(2,1)}, bf16[1024,256]{1,0:T(8,128)(2,1)S(1)}, u32[]{:S(2)}, u32[]{:S(2)}) collective-permute-start(bf16[1024,256]{1,0:T(8,128)(2,1)} %slice.31.refs_2_), channel_id=1, source_target_pairs={{0,96},{8,104},{16,112},{24,120},{32,0},{40,8},{48,16},{56,24},{64... | collective-permute-start | bytes 1572872 | tf_op jit(solution)/shard_map/ppermute | solution.py:244
  48.9 25.6 %collective-permute-start.2 = (bf16[1024,256]{1,0:T(8,128)(2,1)}, bf16[1024,256]{1,0:T(8,128)(2,1)S(1)}, u32[]{:S(2)}, u32[]{:S(2)}) collective-permute-start(bf16[1024,256]{1,0:T(8,128)(2,1)} %slice.31.refs_2_), channel_id=1, source_target_pairs={{0,32},{8,40},{16,48},{24,56},{32,64},{40,72},{48,80},{56,88},{64,... | collective-permute-start | bytes 1572872 | tf_op jit(solution)/shard_map/ppermute | solution.py:244
  49.6 24.9 %collective-permute-start.1 = (bf16[1024,256]{1,0:T(8,128)(2,1)}, bf16[1024,256]{1,0:T(8,128)(2,1)S(1)}, u32[]{:S(2)}, u32[]{:S(2)}) collective-permute-start(bf16[1024,256]{1,0:T(8,128)(2,1)} %slice.31.refs_2_), channel_id=1, source_target_pairs={{0,16},{8,24},{16,0},{24,8},{32,48},{40,56},{48,32},{56,40},{64,80... | collective-permute-start | bytes 1572872 | tf_op jit(solution)/shard_map/ppermute | solution.py:244
  74.5 3.1 %collective-permute-start.4 = (bf16[1024,256]{1,0:T(8,128)(2,1)S(1)}, bf16[1024,256]{1,0:T(8,128)(2,1)S(1)}, u32[]{:S(2)}, u32[]{:S(2)}) collective-permute-start(bf16[1024,256]{1,0:T(8,128)(2,1)S(1)} %get-tuple-element.24.refs_4_), channel_id=1, source_target_pairs={{0,8},{8,0},{16,24},{24,16},{32,40},{40,32},{48,56},{56,48},{64,72... | collective-permute-start | bytes 1572872 | tf_op jit(solution)/shard_map/ppermute | solution.py:244
  75.4 34.9 %collective-permute-start.8 = (bf16[1024,256]{1,0:T(8,128)(2,1)S(1)}, bf16[1024,256]{1,0:T(8,128)(2,1)S(1)}, u32[]{:S(2)}, u32[]{:S(2)}) collective-permute-start(bf16[1024,256]{1,0:T(8,128)(2,1)S(1)} %get-tuple-element.24.refs_4_), channel_id=1, source_target_pairs={{0,96},{8,104},{16,112},{24,120},{32,0},{40,8},{48,16},{56,24},{64... | collective-permute-start | bytes 1572872 | tf_op jit(solution)/shard_map/ppermute | solution.py:244
  77.1 33.2 %collective-permute-start.7 = (bf16[1024,256]{1,0:T(8,128)(2,1)S(1)}, bf16[1024,256]{1,0:T(8,128)(2,1)S(1)}, u32[]{:S(2)}, u32[]{:S(2)}) collective-permute-start(bf16[1024,256]{1,0:T(8,128)(2,1)S(1)} %get-tuple-element.24.refs_4_), channel_id=1, source_target_pairs={{0,32},{8,40},{16,48},{24,56},{32,64},{40,72},{48,80},{56,88},{64,... | collective-permute-start | bytes 1572872 | tf_op jit(solution)/shard_map/ppermute | solution.py:244
  77.1 36.9 %collective-permute-start.6 = (bf16[1024,256]{1,0:T(8,128)(2,1)S(1)}, bf16[1024,256]{1,0:T(8,128)(2,1)S(1)}, u32[]{:S(2)}, u32[]{:S(2)}) collective-permute-start(bf16[1024,256]{1,0:T(8,128)(2,1)S(1)} %get-tuple-element.26.refs_7_), channel_id=1, source_target_pairs={{0,8},{8,0},{16,24},{24,16},{32,40},{40,32},{48,56},{56,48},{64,72... | collective-permute-start | bytes 1572872 | tf_op jit(solution)/shard_map/ppermute | solution.py:244
  77.6 32.7 %collective-permute-start.5 = (bf16[1024,256]{1,0:T(8,128)(2,1)S(1)}, bf16[1024,256]{1,0:T(8,128)(2,1)S(1)}, u32[]{:S(2)}, u32[]{:S(2)}) collective-permute-start(bf16[1024,256]{1,0:T(8,128)(2,1)S(1)} %get-tuple-element.25.refs_6_.refs_3_), channel_id=1, source_target_pairs={{0,8},{8,0},{16,24},{24,16},{32,40},{40,32},{48,56},{56,48},{64,72... | collective-permute-start | bytes 1572872 | tf_op jit(solution)/shard_map/ppermute | solution.py:244
  110.3 36.4 %collective-permute-start.12 = (bf16[1024,256]{1,0:T(8,128)(2,1)S(1)}, bf16[1024,256]{1,0:T(8,128)(2,1)S(1)}, u32[]{:S(2)}, u32[]{:S(2)}) collective-permute-start(bf16[1024,256]{1,0:T(8,128)(2,1)S(1)} %get-tuple-element.30.refs_7_), channel_id=1, source_target_pairs={{0,96},{8,104},{16,112},{24,120},{32,0},{40,8},{48,16},{56,24},{64... | collective-permute-start | bytes 1572872 | tf_op jit(solution)/shard_map/ppermute | solution.py:244
  113.2 34.2 %collective-permute-start.10 = (bf16[1024,256]{1,0:T(8,128)(2,1)S(1)}, bf16[1024,256]{1,0:T(8,128)(2,1)S(1)}, u32[]{:S(2)}, u32[]{:S(2)}) collective-permute-start(bf16[1024,256]{1,0:T(8,128)(2,1)S(1)} %get-tuple-element.30.refs_7_), channel_id=1, source_target_pairs={{0,8},{8,0},{16,24},{24,16},{32,40},{40,32},{48,56},{56,48},{64,72... | collective-permute-start | bytes 1572872 | tf_op jit(solution)/shard_map/ppermute | solution.py:244
  114.0 32.7 %collective-permute-start.11 = (bf16[1024,256]{1,0:T(8,128)(2,1)S(1)}, bf16[1024,256]{1,0:T(8,128)(2,1)S(1)}, u32[]{:S(2)}, u32[]{:S(2)}) collective-permute-start(bf16[1024,256]{1,0:T(8,128)(2,1)S(1)} %get-tuple-element.33), channel_id=1, source_target_pairs={{0,32},{8,40},{16,48},{24,56},{32,64},{40,72},{48,80},{56,88},{64,... | collective-permute-start | bytes 1572872 | tf_op jit(solution)/shard_map/ppermute | solution.py:244
  114.0 33.4 %collective-permute-start.9 = (bf16[1024,256]{1,0:T(8,128)(2,1)S(1)}, bf16[1024,256]{1,0:T(8,128)(2,1)S(1)}, u32[]{:S(2)}, u32[]{:S(2)}) collective-permute-start(bf16[1024,256]{1,0:T(8,128)(2,1)S(1)} %get-tuple-element.29.refs_6_), channel_id=1, source_target_pairs={{0,8},{8,0},{16,24},{24,16},{32,40},{40,32},{48,56},{56,48},{64,72... | collective-permute-start | bytes 1572872 | tf_op jit(solution)/shard_map/ppermute | solution.py:244
  146.7 2.1 collective-permute-start.13
  147.3 2.3 %collective-permute-start.14 = (bf16[1024,256]{1,0:T(8,128)(2,1)S(1)}, bf16[1024,256]{1,0:T(8,128)(2,1)S(1)}, u32[]{:S(2)}, u32[]{:S(2)}) collective-permute-start(bf16[1024,256]{1,0:T(8,128)(2,1)S(1)} %get-tuple-element.35.refs_7_), channel_id=1, source_target_pairs={{0,8},{8,0},{16,24},{24,16},{32,40},{40,32},{48,56},{56,48},{64,72... | collective-permute-start | bytes 1572872 | tf_op jit(solution)/shard_map/ppermute | solution.py:244
